TPU v7x, 512 devices: a whole 4x4x16 slice. The times are simulated.
512 devices in a mesh: freq: 8 (over y, core), pair: 64 (over z, x).
Axes of the slice: x: 4, y: 4, z: 16, core: 2. Of those that a mesh axis runs over, the one named last changes fastest.
Arguments:
- vertex: bfloat16 [1920, 128, 128], P('pair', 'freq'), may hold values from -1.5 to 1.5
- deriv_s: bfloat16 [1920, 128, 128], P('pair', None, 'freq'), may hold values from -1.1953125 to 1.1953125
- deriv_u: bfloat16 [1920, 128, 128], P('pair', None, 'freq'), may hold values from -1.1953125 to 1.1953125
- freq_map_s: int32 [128], replicated, may hold values from 0 to 127, each once
- freq_map_u: int32 [128], replicated, may hold values from 0 to 127, each once
- pair_sym: int32 [1920], P('pair'), may hold values from 0 to 1919, as said below
- propagator: float32 [128], replicated, may hold values from 0.1 to 1
- left_pairs: int32 [1920, 56], P('pair'), may hold values from 0 to 1919, as said below
- right_pairs: int32 [1920, 56], P('pair'), may hold values from 0 to 1919, as said below
- lengths: int32 [1920], P('pair'), may hold values from 1 to 56
Outputs:
- correction: float32 [1920, 128, 128], P('pair', 'freq')
Inputs may be any that keep to these rules, and one draw needn't show every extreme that they name: pair_sym is a permutation of each aligned block of 30 pairs onto itself. For pair r in block b = r // 30, left_pairs[r, k] lies in blocks b - 1, b or b + 1 of 30 pairs. For pair r in block b = r // 30, right_pairs[r, k] lies in blocks b - 1, b or b + 1 of 30 pairs, and the 56 entries of one row are distinct.
All inputs are finite; a program needn't handle non-finite values.
Results may differ from a plain program's by a relative error of at most 0.0042.
Values may be sent and summed in bfloat16 or wider, within the bound.
A program may use at most 64 MiB of HBM per device.

v0:
```python
import functools

import jax
import jax.numpy as jnp
from jax import lax
from jax.experimental import pallas as pl
from jax.experimental.pallas import tpu as pltpu
from jax.sharding import PartitionSpec as P

MESH = pl.DeviceIdType.MESH
BF16 = jnp.bfloat16
F32 = jnp.float32

BEFORE, OWN, AFTER = 0, 1, 2
VERTEX, DERIV = 0, 1
PARTS = 6


def regroup(parts):
    count = len(parts)
    rows, lanes = parts[0].shape
    width = lanes // count
    lane = lax.broadcasted_iota(jnp.int32, (rows, lanes), 1)
    parts = list(parts)
    step = 1
    while step < count:
        high = (lane & (width * step)) != 0
        for q in range(count):
            if (q // step) % 2 == 0:
                a, b = parts[q], parts[q + step]
                parts[q] = jnp.where(high, pltpu.roll(b, width * step, 1), a)
                parts[q + step] = jnp.where(high, b, pltpu.roll(a, lanes - width * step, 1))
        step *= 2
    return parts


def kernel(
    dims,
    v_in,
    s_in,
    u_in,
    map_s_in,
    map_u_in,
    prop_in,
    left_in,
    right_in,
    sym_in,
    len_in,
    out,
    s_ref,
    u_ref,
    map_s_ref,
    map_u_ref,
    prop_ref,
    left_ref,
    right_ref,
    sym_ref,
    len_ref,
    out_ref,
    right,
    packed,
    spread,
    lefts,
    chunks,
    columns,
    table,
    sums,
    part_out,
    part_in,
    sel_vec,
    sel,
    recv_right,
    recv_spread,
    recv_beside,
    recv_cols,
    recv_part,
    send_part,
    send,
    local,
):
    n_freq, n_pair = dims
    n_chip = n_freq // 2
    pairs, rows, nf = v_in.shape
    slots = left_ref.shape[1]
    freq, block = lax.axis_index("freq"), lax.axis_index("pair")
    chip, core = freq // 2, freq % 2

    sibling = (freq + 1 - 2 * core, block)
    x_up = (freq, (block + 1) % n_pair)
    x_down = (freq, (block + n_pair - 1) % n_pair)

    def own(kind, slot=OWN, of=core):
        return right.at[kind, of, slot * pairs : (slot + 1) * pairs]

    barrier = pltpu.get_barrier_semaphore()
    peers = [((freq + o) % n_freq, block) for o in range(1, n_freq)] + [x_up, x_down]
    for peer in peers:
        pl.semaphore_signal(barrier, inc=1, device_id=peer, device_id_type=MESH)
    loads = [
        pltpu.make_async_copy(src, dst, local.at[i])
        for i, (src, dst) in enumerate(
            (
                (v_in, own(VERTEX)),
                (sym_in, sym_ref),
                (s_in, s_ref),
                (u_in, u_ref),
                (map_s_in, map_s_ref),
                (map_u_in, map_u_ref),
                (prop_in, prop_ref),
                (left_in, left_ref),
                (right_in, right_ref),
                (len_in, len_ref),
            )
        )
    ]
    for load in loads:
        load.start()

    sent = []

    def push(src, dst, recv_sem, peer):
        copy = pltpu.make_async_remote_copy(
            src_ref=src,
            dst_ref=dst,
            send_sem=send.at[len(sent)],
            recv_sem=recv_sem,
            device_id=peer,
            device_id_type=MESH,
        )
        copy.start()
        sent.append(copy)

    def arrive(ref, recv_sem):
        pltpu.make_async_remote_copy(
            src_ref=ref,
            dst_ref=ref,
            send_sem=send.at[0],
            recv_sem=recv_sem,
            device_id=sibling,
            device_id_type=MESH,
        ).wait_recv()

    def push_beside(kind):
        push(own(kind), own(kind, BEFORE), recv_right.at[kind, core, BEFORE], x_up)
        push(own(kind), own(kind, AFTER), recv_right.at[kind, core, AFTER], x_down)

    def push_sibling(kind, slot):
        push(own(kind, slot), own(kind, slot), recv_right.at[kind, core, slot], sibling)

    n_packed = packed.shape[2]
    zero_rows = jnp.zeros((rows, nf), BF16)

    def pack_left(kind):
        for g in range(n_packed):
            four = [
                right[kind, core, OWN * pairs + p] if p < pairs else zero_rows
                for p in range(n_chip * g, n_chip * (g + 1))
            ]
            for c, tile in enumerate(regroup(four)):
                packed[kind, c, g] = tile
        spread[OWN, kind, chip] = packed[kind, chip]

    def push_left(kind):
        for o in (2, 1, 3):
            c = (chip + o) % n_chip
            push(
                packed.at[kind, c],
                spread.at[OWN, kind, chip],
                recv_spread.at[kind, chip],
                (2 * c + core, block),
            )

    def pass_chunk_on(kind, c):
        at = spread.at[OWN, kind, c]
        push(at, spread.at[BEFORE, kind, c], recv_beside.at[kind, BEFORE, c], x_up)
        push(at, spread.at[AFTER, kind, c], recv_beside.at[kind, AFTER, c], x_down)

    def pass_left_on(kind):
        for o in (1, 3, 2):
            c = (chip + o) % n_chip
            arrive(spread.at[OWN, kind, c], recv_spread.at[kind, c])
            pass_chunk_on(kind, c)

    def left_arrives(kind, slot):
        for o in (0, 1, 3, 2):
            c = (chip + o) % n_chip
            arrive(spread.at[slot, kind, c], recv_beside.at[kind, slot, c])

    loads[0].wait()
    pack_left(VERTEX)
    for load in loads[1:4]:
        load.wait()
    group = nf // rows
    n_groups = columns.shape[2]
    for kind in (0, 1):
        for g in range(n_groups):
            eight = []
            for p in range(g * group, (g + 1) * group):
                if p >= pairs:
                    eight.append(zero_rows)
                elif kind == 0:
                    eight.append(s_ref[p])
                else:
                    eight.append(u_ref[lax.rem(sym_ref[p], pairs)])
            for f, tile in enumerate(regroup(eight)):
                chunks[f, kind, g] = tile
    columns[freq] = chunks[freq]

    pl.semaphore_wait(barrier, len(peers))
    push_left(VERTEX)
    push_beside(VERTEX)
    pass_chunk_on(VERTEX, chip)
    for o in (4, 3, 5, 2, 6, 1, 7):
        f = (freq + o) % n_freq
        push(chunks.at[f], columns.at[freq], recv_cols.at[freq], (f, block))
    push_sibling(VERTEX, OWN)

    for load in loads[4:]:
        load.wait()
    wide = lax.broadcasted_iota(jnp.int32, (nf, nf), 0)
    table[0:nf, :] = jnp.where(wide == map_s_ref[...], 1.0, 0.0).astype(BF16)
    table[nf : 2 * nf, :] = jnp.where(wide == map_u_ref[...], 1.0, 0.0).astype(BF16)
    window_first = (block - 1) * pairs
    row_id = lax.broadcasted_iota(jnp.int32, (pairs, slots), 0)
    slot_id = lax.broadcasted_iota(jnp.int32, (pairs, slots), 1)
    count = jnp.zeros((pairs, slots), jnp.int32)
    for r in range(pairs):
        count = jnp.where(row_id == r, len_ref[r], count)
    target = jnp.where(slot_id < count, right_ref[...] - window_first, -1)
    source = left_ref[...] - window_first
    stride = n_chip * n_packed
    gap = stride - pairs
    source = source + 1 + jnp.where(source >= pairs, gap, 0) + jnp.where(source >= 2 * pairs, gap, 0)
    lanes = lax.broadcasted_iota(jnp.int32, (pairs, nf), 1)
    chosen = jnp.zeros((pairs, nf), jnp.int32)
    for k in range(slots):
        chosen = jnp.where(target[:, k : k + 1] == lanes, source[:, k : k + 1], chosen)
    sel_vec[...] = chosen
    to_scalar = pltpu.make_async_copy(sel_vec, sel, local.at[10])
    to_scalar.start()

    width = nf // n_chip
    tile_lane = lax.broadcasted_iota(jnp.int32, (rows, nf), 1)
    wide_prop = jnp.broadcast_to(prop_ref[...], (rows, nf))
    tiles = regroup([wide_prop] * n_chip)
    prop = tiles[0]
    for c in range(1, n_chip):
        prop = jnp.where(chip == c, tiles[c], prop)

    for half in (0, 1):
        lefts[half, 0] = jnp.zeros(lefts.shape[2:], BF16)
    zones = [
        (tile_lane >= width * z) & (tile_lane < width * (z + 1)) for z in range(n_chip)
    ]

    def fill_lefts(kind, slot):
        def one(g, carry):
            for c in range(n_chip):
                tile = (spread[slot, kind, c, g].astype(F32) * prop).astype(BF16)
                turned = [tile] + [pltpu.roll(tile, width * k, 1) for k in range(1, n_chip)]
                for q in range(n_chip):
                    at = 1 + slot * stride + g * n_chip + q
                    for half in (0, 1):
                        zone = 2 * half + kind
                        rest = jnp.zeros((rows, nf), BF16) if kind == VERTEX else lefts[half, at, c]
                        lefts[half, at, c] = jnp.where(zones[zone], turned[(zone - q) % n_chip], rest)
            return carry

        lax.fori_loop(0, n_packed, one, 0)

    pass_left_on(VERTEX)

    for o in range(1, n_freq):
        f = (freq + o) % n_freq
        arrive(columns.at[f], recv_cols.at[f])
    for g in range(n_groups):
        cols = jnp.concatenate([columns[:, kind, g].reshape(nf, nf) for kind in (0, 1)], axis=0)
        rows_t = lax.dot_general(
            cols, table[...], (((0,), (0,)), ((), ())), preferred_element_type=F32
        ).astype(BF16)
        n = min(group, pairs - g * group)
        start = OWN * pairs + g * group
        right[DERIV, core, start : start + n] = rows_t.reshape(group, rows, nf)[:n]
    pack_left(DERIV)
    push_left(DERIV)
    pass_chunk_on(DERIV, chip)
    push_beside(DERIV)
    push_sibling(DERIV, OWN)

    for slot in (BEFORE, AFTER):
        arrive(own(VERTEX, slot), recv_right.at[VERTEX, core, slot])
        push_sibling(VERTEX, slot)
    fill_lefts(VERTEX, OWN)
    for slot in (BEFORE, AFTER):
        left_arrives(VERTEX, slot)
        fill_lefts(VERTEX, slot)

    pass_left_on(DERIV)
    fill_lefts(DERIV, OWN)
    for slot in (BEFORE, AFTER):
        arrive(own(DERIV, slot), recv_right.at[DERIV, core, slot])
        push_sibling(DERIV, slot)
    for slot in (BEFORE, AFTER):
        left_arrives(DERIV, slot)
        fill_lefts(DERIV, slot)
    other = 1 - core
    for slot in (OWN, BEFORE, AFTER):
        for kind in (VERTEX, DERIV):
            arrive(own(kind, slot, other), recv_right.at[kind, other, slot])

    to_scalar.wait()
    size = pairs // PARTS
    tall = n_chip * rows

    def part_copy(part, o):
        c = (chip + o) % n_chip
        return pltpu.make_async_remote_copy(
            src_ref=part_out.at[part, o],
            dst_ref=part_in.at[part, chip],
            send_sem=send_part.at[part, o],
            recv_sem=recv_part.at[part, chip],
            device_id=(2 * c + core, block),
            device_id_type=MESH,
        )

    def one_part(part, carry):
        first_row = part * size
        lhs, rhs = [], []
        for q in range(0, 3 * pairs, 2):
            lhs.append(
                jnp.concatenate(
                    [
                        (
                            lefts[0, sel[first_row + r, q]] + lefts[1, sel[first_row + r, q + 1]]
                        ).reshape(tall, nf)
                        for r in range(size)
                    ],
                    axis=0,
                )
            )
            for p in (q, q + 1):
                rhs += [right[kind, :, p].reshape(2 * rows, nf) for kind in (DERIV, VERTEX)]
        terms = jnp.dot(
            jnp.concatenate(lhs, axis=1),
            jnp.concatenate(rhs, axis=0),
            preferred_element_type=F32,
        )
        sums[...] = terms.reshape(size, n_chip, rows, nf)
        out_ref[pl.ds(first_row, size)] = sums[:, chip]
        for o in (2, 1, 3):
            part_out[part, o] = sums[:, (chip + o) % n_chip].astype(BF16)
            part_copy(part, o).start()
        return carry

    lax.fori_loop(0, PARTS, one_part, 0)
    stores = []
    for part in range(PARTS):
        at = slice(part * size, (part + 1) * size)
        total = out_ref[at]
        for o in (1, 3, 2):
            c = (chip + o) % n_chip
            arrive(part_in.at[part, c], recv_part.at[part, c])
            total = total + part_in[part, c].astype(F32)
        out_ref[at] = total
        stores.append(pltpu.make_async_copy(out_ref.at[at], out.at[at], local.at[part]))
        stores[-1].start()
    for part in range(PARTS):
        for o in (2, 1, 3):
            part_copy(part, o).wait_send()
    for store in stores:
        store.wait()
    for copy in sent:
        copy.wait_send()


def per_device(
    dims,
    vertex,
    deriv_s,
    deriv_u,
    freq_map_s,
    freq_map_u,
    pair_sym,
    propagator,
    left_pairs,
    right_pairs,
    lengths,
):
    n_freq, _ = dims
    n_chip = n_freq // 2
    pairs, rows, nf = vertex.shape
    n_groups = -(-pairs * rows // nf)
    n_packed = -(-pairs // n_chip)
    size = pairs // PARTS
    hbm = pl.BlockSpec(memory_space=pltpu.HBM)
    dma = pltpu.SemaphoreType.DMA
    return pl.pallas_call(
        functools.partial(kernel, dims),
        out_shape=jax.ShapeDtypeStruct((pairs, rows, nf), F32),
        in_specs=[hbm] * 10,
        out_specs=hbm,
        scratch_shapes=[
            pltpu.VMEM((pairs, rows, nf), BF16),
            pltpu.VMEM((pairs, rows, nf), BF16),
            pltpu.VMEM((1, nf), jnp.int32),
            pltpu.VMEM((1, nf), jnp.int32),
            pltpu.VMEM((1, nf), F32),
            pltpu.VMEM(left_pairs.shape, jnp.int32),
            pltpu.VMEM(right_pairs.shape, jnp.int32),
            pltpu.SMEM(pair_sym.shape, jnp.int32),
            pltpu.SMEM(lengths.shape, jnp.int32),
            pltpu.VMEM((pairs, rows, nf), F32),
            pltpu.VMEM((2, 2, 3 * pairs, rows, nf), BF16),
            pltpu.VMEM((2, n_chip, n_packed, rows, nf), BF16),
            pltpu.VMEM((3, 2, n_chip, n_packed, rows, nf), BF16),
            pltpu.VMEM((2, 1 + 3 * n_packed * n_chip, n_chip, rows, nf), BF16),
            pltpu.VMEM((n_freq, 2, n_groups, rows, nf), BF16),
            pltpu.VMEM((n_freq, 2, n_groups, rows, nf), BF16),
            pltpu.VMEM((2 * nf, nf), BF16),
            pltpu.VMEM((size, n_chip, rows, nf), F32),
            pltpu.VMEM((PARTS, n_chip, size, rows, nf), BF16),
            pltpu.VMEM((PARTS, n_chip, size, rows, nf), BF16),
            pltpu.VMEM((pairs, nf), jnp.int32),
            pltpu.SMEM((pairs, nf), jnp.int32),
            dma((2, 2, 3)),
            dma((2, n_chip)),
            dma((2, 3, n_chip)),
            dma((n_freq,)),
            dma((PARTS, n_chip)),
            dma((PARTS, n_chip)),
            dma((64,)),
            dma((11,)),
        ],
        compiler_params=pltpu.CompilerParams(
            collective_id=0, has_side_effects=True, vmem_limit_bytes=63 * 1024 * 1024
        ),
    )(
        vertex,
        jnp.swapaxes(deriv_s, 1, 2),
        jnp.swapaxes(deriv_u, 1, 2),
        freq_map_s.reshape(1, nf),
        freq_map_u.reshape(1, nf),
        propagator.reshape(1, nf),
        left_pairs,
        right_pairs,
        pair_sym,
        lengths,
    )


def solution(mesh):
    dims = (mesh.shape["freq"], mesh.shape["pair"])
    return jax.shard_map(
        functools.partial(per_device, dims),
        mesh=mesh,
        in_specs=(
            P("pair", "freq", None),
            P("pair", None, "freq"),
            P("pair", None, "freq"),
            P(),
            P(),
            P("pair"),
            P(),
            P("pair", None),
            P("pair", None),
            P("pair"),
        ),
        out_specs=P("pair", "freq", None),
        check_vma=False,
    )
```

profile of v0, /device:TPU:1, one launch (start us, length us, event | category | flops | bytes accessed | tf_op | source)
XLA Modules:
  0.0 45.5 jit_solution(4229523080695438647)
XLA Ops:
  0.0 43.8 %shard_map.100 = f32[30,16,128]{2,1,0:T(8,128)} custom-call(bf16[30,16,128]{2,1,0:T(8,128)(2,1)} %v_in.1, bf16[30,16,128]{2,1,0:T(8,128)(2,1)} %bitcast.5, bf16[30,16,128]{2,1,0:T(8,128)(2,1)} %bitcast.6, s32[1,128]{1,0:T(1,128)} %bitcast.7, s32[1,128]{1,0:T(1,128)} %bitcast.8, f32[1,128]{1,0:T(1,128)} %bitcast.9, s32[30,56]{1,0:T(8,128)} %left_in.1, ...), custom_call_target="tpu_custom_call" | custom-call | tf_op jit(solution)/shard_map/pallas_call | solution.py:397
  43.8 1.7 %copy.12 = f32[30,16,128]{2,1,0:T(8,128)} copy(f32[30,16,128]{2,1,0:T(8,128)} %shard_map.100) | data formatting | bytes 491520
where the time goes:
time: 45.6 us; the launch traced here: 45.5 us
  Pallas kernels  43.8 us (96%)
  local copies, waits for them, and re-layouts  1.65 us (4%)
    pallas_call x1, Pallas kernels, per_device(): pl.pallas_call(functools.partial(kernel, dims), out_shape=jax.ShapeDtypeS...  43.8 us
    unnamed x1, local copies, waits for them, and re-layouts  1.65 us

commit v1 on v0

--- a/solution.py
+++ b/solution.py
@@ -254,7 +254,7 @@
     ]
 
     def fill_lefts(kind, slot):
-        def one(g, carry):
+        for g in range(n_packed):
             for c in range(n_chip):
                 tile = (spread[slot, kind, c, g].astype(F32) * prop).astype(BF16)
                 turned = [tile] + [pltpu.roll(tile, width * k, 1) for k in range(1, n_chip)]
@@ -262,11 +262,8 @@
                     at = 1 + slot * stride + g * n_chip + q
                     for half in (0, 1):
                         zone = 2 * half + kind
-                        rest = jnp.zeros((rows, nf), BF16) if kind == VERTEX else lefts[half, at, c]
+                        rest = zero_rows if kind == VERTEX else lefts[half, at, c]
                         lefts[half, at, c] = jnp.where(zones[zone], turned[(zone - q) % n_chip], rest)
-            return carry
-
-        lax.fori_loop(0, n_packed, one, 0)
 
     pass_left_on(VERTEX)
 

time: 45.6 us -> 44.6 us (0.978)
  Pallas kernels: 43.8 us -> 42.8 us
    pallas_call x1, Pallas kernels: 43.8 us -> 42.8 us  [per_device(): pl.pallas_call(functools.partial(kernel, dims), out_shape=jax.ShapeDtypeS...]
where the time goes in v1:
time: 44.6 us; the launch traced here: 44.5 us
  Pallas kernels  42.8 us (96%)
  local copies, waits for them, and re-layouts  1.65 us (4%)
    pallas_call x1, Pallas kernels, per_device(): pl.pallas_call(functools.partial(kernel, dims), out_shape=jax.ShapeDtypeS...  42.8 us
    unnamed x1, local copies, waits for them, and re-layouts  1.65 us

profile of v1, /device:TPU:1, one launch (start us, length us, event | category | flops | bytes accessed | tf_op | source)
XLA Modules:
  0.0 44.5 jit_solution(11663453606625190153)
XLA Ops:
  0.0 42.8 %shard_map.100 = f32[30,16,128]{2,1,0:T(8,128)} custom-call(bf16[30,16,128]{2,1,0:T(8,128)(2,1)} %v_in.1, bf16[30,16,128]{2,1,0:T(8,128)(2,1)} %bitcast.5, bf16[30,16,128]{2,1,0:T(8,128)(2,1)} %bitcast.6, s32[1,128]{1,0:T(1,128)} %bitcast.7, s32[1,128]{1,0:T(1,128)} %bitcast.8, f32[1,128]{1,0:T(1,128)} %bitcast.9, s32[30,56]{1,0:T(8,128)} %left_in.1, ...), custom_call_target="tpu_custom_call" | custom-call | tf_op jit(solution)/shard_map/pallas_call | solution.py:394
  42.8 1.7 %copy.12 = f32[30,16,128]{2,1,0:T(8,128)} copy(f32[30,16,128]{2,1,0:T(8,128)} %shard_map.100) | data formatting | bytes 491520

commit v2 on v1

--- a/solution.py
+++ b/solution.py
@@ -253,9 +253,9 @@
         (tile_lane >= width * z) & (tile_lane < width * (z + 1)) for z in range(n_chip)
     ]
 
-    def fill_lefts(kind, slot):
+    def fill_lefts(kind, slot, chips=range(n_chip)):
         for g in range(n_packed):
-            for c in range(n_chip):
+            for c in chips:
                 tile = (spread[slot, kind, c, g].astype(F32) * prop).astype(BF16)
                 turned = [tile] + [pltpu.roll(tile, width * k, 1) for k in range(1, n_chip)]
                 for q in range(n_chip):
@@ -297,9 +297,11 @@
     for slot in (BEFORE, AFTER):
         arrive(own(DERIV, slot), recv_right.at[DERIV, core, slot])
         push_sibling(DERIV, slot)
-    for slot in (BEFORE, AFTER):
-        left_arrives(DERIV, slot)
-        fill_lefts(DERIV, slot)
+    for o in (0, 1, 3, 2):
+        c = (chip + o) % n_chip
+        for slot in (BEFORE, AFTER):
+            arrive(spread.at[slot, DERIV, c], recv_beside.at[DERIV, slot, c])
+            fill_lefts(DERIV, slot, (c,))
     other = 1 - core
     for slot in (OWN, BEFORE, AFTER):
         for kind in (VERTEX, DERIV):

time: 44.6 us -> 44.5 us (level)
  no operation moved by 1% of the time
where the time goes in v2:
time: 44.5 us; the launch traced here: 44.3 us
  Pallas kernels  42.6 us (96%)
  local copies, waits for them, and re-layouts  1.65 us (4%)
    pallas_call x1, Pallas kernels, per_device(): pl.pallas_call(functools.partial(kernel, dims), out_shape=jax.ShapeDtypeS...  42.6 us
    unnamed x1, local copies, waits for them, and re-layouts  1.65 us

profile of v2, /device:TPU:1, one launch (start us, length us, event | category | flops | bytes accessed | tf_op | source)
XLA Modules:
  0.0 44.3 jit_solution(12939195849856929234)
XLA Ops:
  0.0 42.6 %shard_map.100 = f32[30,16,128]{2,1,0:T(8,128)} custom-call(bf16[30,16,128]{2,1,0:T(8,128)(2,1)} %v_in.1, bf16[30,16,128]{2,1,0:T(8,128)(2,1)} %bitcast.5, bf16[30,16,128]{2,1,0:T(8,128)(2,1)} %bitcast.6, s32[1,128]{1,0:T(1,128)} %bitcast.7, s32[1,128]{1,0:T(1,128)} %bitcast.8, f32[1,128]{1,0:T(1,128)} %bitcast.9, s32[30,56]{1,0:T(8,128)} %left_in.1, ...), custom_call_target="tpu_custom_call" | custom-call | tf_op jit(solution)/shard_map/pallas_call | solution.py:396
  42.6 1.7 %copy.12 = f32[30,16,128]{2,1,0:T(8,128)} copy(f32[30,16,128]{2,1,0:T(8,128)} %shard_map.100) | data formatting | bytes 491520

commit v3 on v1

--- a/solution.py
+++ b/solution.py
@@ -13,7 +13,7 @@
 
 BEFORE, OWN, AFTER = 0, 1, 2
 VERTEX, DERIV = 0, 1
-PARTS = 6
+PARTS = 5
 
 
 def regroup(parts):

time: 44.6 us -> 44.2 us (level)
  no operation moved by 1% of the time
where the time goes in v3:
time: 44.2 us; the launch traced here: 44 us
  Pallas kernels  42.4 us (96%)
  local copies, waits for them, and re-layouts  1.65 us (4%)
    pallas_call x1, Pallas kernels, per_device(): pl.pallas_call(functools.partial(kernel, dims), out_shape=jax.ShapeDtypeS...  42.4 us
    unnamed x1, local copies, waits for them, and re-layouts  1.65 us

profile of v3, /device:TPU:1, one launch (start us, length us, event | category | flops | bytes accessed | tf_op | source)
XLA Modules:
  0.0 44.0 jit_solution(4772495184687214548)
XLA Ops:
  0.0 42.4 %shard_map.100 = f32[30,16,128]{2,1,0:T(8,128)} custom-call(bf16[30,16,128]{2,1,0:T(8,128)(2,1)} %v_in.1, bf16[30,16,128]{2,1,0:T(8,128)(2,1)} %bitcast.5, bf16[30,16,128]{2,1,0:T(8,128)(2,1)} %bitcast.6, s32[1,128]{1,0:T(1,128)} %bitcast.7, s32[1,128]{1,0:T(1,128)} %bitcast.8, f32[1,128]{1,0:T(1,128)} %bitcast.9, s32[30,56]{1,0:T(8,128)} %left_in.1, ...), custom_call_target="tpu_custom_call" | custom-call | tf_op jit(solution)/shard_map/pallas_call | solution.py:394
  42.4 1.7 %copy.12 = f32[30,16,128]{2,1,0:T(8,128)} copy(f32[30,16,128]{2,1,0:T(8,128)} %shard_map.100) | data formatting | bytes 491520
